TPU v7x, 512 devices: a whole 4x8x8 slice. The times are simulated.
512 devices in a mesh: row: 16 (over z, core), col: 32 (over y, x).
Axes of the slice: x: 4, y: 8, z: 8, core: 2. Of those that a mesh axis runs over, the one named last changes fastest.
Arguments:
- grad: float32 [2048, 53248], P('row', 'col'), may hold values from -15 to 15
- momentum: float32 [2048, 53248], P('row', 'col'), may hold values from -6 to 6
- factor: float32 [53248, 256], P(('col', 'row')), may hold values from -0.02734375 to 0.02734375
Outputs:
- update: float32 [2048, 53248], P('row', 'col')
- momentum_out: float32 [2048, 53248], P('row', 'col')
- factor_out: float32 [53248, 256], P(('col', 'row'))
All inputs are finite; a program needn't handle non-finite values.
Results may differ from a plain program's by a relative error of at most 0.000098.
Values sent between devices are 32-bit elements; how exact they have to be, the bound alone decides.
A program may use at most 64 MiB of HBM per device.

v0:
```python
import math

import jax
import jax.numpy as jnp
from jax import lax
from jax.sharding import PartitionSpec as P

feedback = 0.05
epsilon = 1e-06


def per_device(grad, momentum, factor):
    highest = lax.Precision.HIGHEST
    summed = momentum + grad
    row_count = summed.shape[0]
    col_count = summed.shape[1]
    rank_width = factor.shape[1]
    local_factor = lax.all_gather(factor, "row", axis=0, tiled=True)
    partial_left = jnp.dot(
        summed, local_factor, precision=highest, preferred_element_type=jnp.float32
    )
    left = lax.psum(partial_left, "col")
    gram_part = jnp.dot(left.T, left, precision=highest, preferred_element_type=jnp.float32)
    gram_matrix = lax.psum(gram_part, "row")
    lower_factor = jnp.linalg.cholesky(gram_matrix)
    left_basis = jax.scipy.linalg.solve_triangular(lower_factor, left.T, lower=True).T
    partial_right = lax.dot_general(
        summed,
        left_basis,
        (((0,), (0,)), ((), ())),
        precision=highest,
        preferred_element_type=jnp.float32,
    )
    right_factor = lax.psum(partial_right, "row")
    square_sums = lax.psum(jnp.sum(right_factor * right_factor, axis=0), "col")
    new_factor = right_factor / (jnp.sqrt(square_sums) + epsilon)
    owned_count = col_count // lax.axis_size("row")
    factor_out = lax.dynamic_slice_in_dim(
        new_factor, lax.axis_index("row") * owned_count, owned_count, 0
    )
    momentum_out = summed - feedback * jnp.dot(
        left_basis, right_factor.T, precision=highest, preferred_element_type=jnp.float32
    )
    total_rows = row_count * lax.axis_size("row")
    total_cols = col_count * lax.axis_size("col")
    multiplier = math.sqrt(total_rows * total_cols / rank_width)
    update = multiplier * jnp.dot(
        left_basis, new_factor.T, precision=highest, preferred_element_type=jnp.float32
    )
    return (update, momentum_out, factor_out)


def solution(mesh):
    return jax.shard_map(
        per_device,
        mesh=mesh,
        in_specs=(P("row", "col"), P("row", "col"), P(("col", "row"), None)),
        out_specs=(P("row", "col"), P("row", "col"), P(("col", "row"), None)),
        check_vma=False,
    )
```

profile of v0, /device:TPU:1, one launch (start us, length us, event | category | flops | bytes accessed | tf_op | source)
XLA Modules:
  0.0 588.7 jit_solution(4292589701706836170)
XLA Ops:
  7.2 0.7 all-gather.2.cloned.1.call-update
  7.9 1.5 add.43
  9.4 49.4 %all-gather.2.cloned.1.call-done = f32[1664,256]{1,0:T(8,128)} async-done(((f32[104,256]{1,0:T(8,128)}), f32[1664,256]{1,0:T(8,128)}) %all-gather.2.cloned.1.call-update) | async-done | bytes 1703952 | tf_op jit(solution)/shard_map/all_gather | solution.py:18
  58.9 3.1 fusion.14
  62.0 146.5 %all-reduce.5.cloned.1.call-done = f32[128,256]{1,0:T(8,128)} async-done(((f32[128,256]{1,0:T(8,128)}), f32[128,256]{1,0:T(8,128)}) %all-reduce.5.cloned.1.call-update) | async-done | bytes 131088 | tf_op jit(solution)/shard_map/psum | solution.py:22
  208.6 2.1 fusion.15
  210.8 118.0 %all-reduce.7.cloned.1.call-done = f32[256,256]{0,1:T(8,128)} async-done(((f32[256,256]{0,1:T(8,128)}), f32[256,256]{0,1:T(8,128)}) %all-reduce.7.cloned.1.call-update) | async-done | bytes 262160 | tf_op jit(solution)/shard_map/psum | solution.py:24
  328.8 1.1 copy.7
  329.9 1.0 fusion.1
  330.9 11.7 %cholesky.50 = f32[128,128]{1,0:T(8,128)S(1)} custom-call(f32[128,128]{1,0:T(8,128)S(1)} %cholesky.118), custom_call_target="Cholesky" | custom-call | tf_op jit(solution)/shard_map/jit(cholesky)/cholesky | solution.py:25
  342.6 9.8 %custom-call.15 = f32[1,128,128]{1,2,0:T(8,128)S(1)} custom-call(f32[1,128,128]{2,1,0:T(8,128)S(1)} %get-tuple-element.24), custom_call_target="InvertDiagBlocksLowerTriangular" | custom-call | tf_op jit(solution)/shard_map/jit(cholesky)/cholesky | solution.py:25
  353.0 11.7 %cholesky.105 = f32[128,128]{1,0:T(8,128)S(1)} custom-call(f32[128,128]{1,0:T(8,128)S(1)} %convolution_subtract_fusion.1), custom_call_target="Cholesky" | custom-call | tf_op jit(solution)/shard_map/jit(cholesky)/cholesky | solution.py:25
  364.7 0.6 compare_reduce_fusion
  366.8 4.1 while.1
  367.5 1.4 bitcast_dynamic-update-slice_fusion.2
  369.5 1.4 bitcast_dynamic-update-slice_fusion.2
  370.9 19.7 %custom-call.16 = f32[2,128,128]{1,2,0:T(8,128)S(1)} custom-call(f32[2,128,128]{2,1,0:T(8,128)S(1)} %get-tuple-element.10), custom_call_target="InvertDiagBlocksLowerTriangular" | custom-call | tf_op jit(solution)/shard_map/jit(_solve_triangular)/triangular_solve | solution.py:26
  391.5 2.7 fusion.2
  394.2 119.6 %all-reduce.9.cloned.1.call-done = f32[1664,256]{1,0:T(8,128)} async-done(((f32[1664,256]{1,0:T(8,128)}), f32[1664,256]{1,0:T(8,128)}) %all-reduce.9.cloned.1.call-update) | async-done | bytes 1703952 | tf_op jit(solution)/shard_map/psum | solution.py:34
  513.8 1.8 multiply_reduce_fusion
  515.6 60.5 %psum.31 = f32[256]{0:T(256)S(1)} all-reduce(f32[256]{0:T(256)S(1)} %multiply_reduce_fusion), channel_id=1, replica_groups=mesh['row'=16,'col'=32] {'col'}, use_global_device_ids=true, to_apply=%region_8.9 | all-reduce | flops 256 | bytes 2048 | tf_op jit(solution)/shard_map/psum | solution.py:35
  576.3 2.6 convolution_multiply_fusion.1
  578.9 0.7 constant_dynamic-slice_fusion.1
  579.6 2.6 fusion
  (30 shorter events, 3.1 us)
Async XLA Ops:
  7.2 51.7 %all-gather.2.cloned.1.call-start = ((), (), s32[]{:S(2)}) async-start(), calls=%async_computation | async-start | bytes 1810432 | tf_op jit(solution)/shard_map/all_gather | solution.py:18
  7.9 200.7 %all-reduce.5.cloned.1.call-start = ((), (), s32[]{:S(2)}) async-start(), calls=%async_computation.1 | async-start | bytes 262144 | tf_op jit(solution)/shard_map/psum | solution.py:22
  62.0 266.8 %all-reduce.7.cloned.1.call-start = ((), (), s32[]{:S(2)}) async-start(), calls=%async_computation.2 | async-start | bytes 524288 | tf_op jit(solution)/shard_map/psum | solution.py:24
  210.7 303.1 %all-reduce.9.cloned.1.call-start = ((), (), s32[]{:S(2)}) async-start(), calls=%async_computation.3 | async-start | bytes 3407872 | tf_op jit(solution)/shard_map/psum | solution.py:34
  329.8 60.7 %copy-start.1 = (f32[128,256]{1,0:T(8,128)S(1)}, f32[128,256]{1,0:T(8,128)}, u32[]{:S(2)}) copy-start(f32[128,256]{1,0:T(8,128)} %all-reduce.5.cloned.1.call-done) | copy-start | bytes 393220
  513.8 62.4 %copy-start = (f32[1664,256]{1,0:T(8,128)S(1)}, f32[1664,256]{1,0:T(8,128)}, u32[]{:S(2)}) copy-start(f32[1664,256]{1,0:T(8,128)} %all-reduce.9.cloned.1.call-done) | copy-start | bytes 5111812
Sparse Core Ops, SparseCore 0:
  10.1 48.6 all-gather.1
  62.9 145.6 all-reduce.4
  211.6 117.1 all-reduce.6
  394.3 119.4 all-reduce.8
where the time goes:
time: 600 us; the launch traced here: 589 us
  waiting for transfers between devices  434 us (72%)
  blocking collectives  60.5 us (10%)
  other arithmetic  58.1 us (10%)
  between operations  15.2 us (3%)
  matrix products  14.4 us (2%)
    psum x1, waiting for transfers between devices, per_device(): left = lax.psum(partial_left, 'col')  147 us
    psum x1, waiting for transfers between devices, per_device(): right_factor = lax.psum(partial_right, 'row')  120 us
    psum x1, waiting for transfers between devices, per_device(): gram_matrix = lax.psum(gram_part, 'row')  118 us
    psum x1, blocking collectives, per_device(): square_sums = lax.psum(jnp.sum(right_factor * right_factor, axis=0), 'col')  60.5 us
    all_gather x1, waiting for transfers between devices, per_device(): local_factor = lax.all_gather(factor, 'row', axis=0, tiled=True)  49.4 us
    another operation x6, other arithmetic, per_device(): lower_factor = jnp.linalg.cholesky(gram_matrix)  34 us
    another operation x3, other arithmetic, per_device(): jax.scipy.linalg.solve_triangular(lower_factor, left.T, lower=True)  19.7 us
  transfers between devices with their start and end apart: 4, of which 4 were waited for; matrix products, arithmetic and copies ran while one was open for 0% of the time, Pallas kernels for 0%

commit v1 on v0

v1 whole, which is shorter than its diff:
```python
import functools
import math

import jax
import jax.numpy as jnp
from jax import lax
from jax.experimental import pallas as pl
from jax.experimental.pallas import tpu as pltpu
from jax.sharding import PartitionSpec as P

feedback = 0.05
epsilon = 1e-06
MESH = pl.DeviceIdType.MESH
HIGHEST = lax.Precision.HIGHEST
F32 = jnp.float32

RANK = 256
HALF = 128
ZN = 8
RN = 16
CN = 32
ROWS = 128
COLS = 1664
OWN = COLS // RN
CHIP = 2 * OWN
SUBS = ((0, 32), (32, 24), (56, 24), (80, 24))
NS = len(SUBS)
CUT = 2
PANEL = 32


def dot(a, b):
    return jnp.dot(a, b, precision=HIGHEST, preferred_element_type=F32)


def dot_t(a, b):
    return lax.dot_general(
        a, b, (((1,), (1,)), ((), ())), precision=HIGHEST, preferred_element_type=F32
    )


def across_rows(x, t):
    return jnp.broadcast_to(x[t : t + 1, :], (8, 128))


def across_lanes(x, t):
    return jnp.broadcast_to(x[:, t : t + 1], (8, 128))


def reciprocal(p):
    r = pltpu.reciprocal(p, approx=True)
    return r * (2.0 - p * r)


def panel_step(k, m_ref, x_ref):
    groups = PANEL // 8
    row = lax.broadcasted_iota(jnp.int32, (8, 128), 0)
    m_halves = [h for h in (0, 1) if 128 * (h + 1) > k]
    x_halves = [h for h in (0, 1) if 128 * h < k + PANEL]
    rows = []
    for g in range(groups):
        at = slice(k + 8 * g, k + 8 * g + 8)
        held = {}
        for h in m_halves:
            held["m", h] = m_ref[h, at, :]
        for h in x_halves:
            held["x", h] = x_ref[h, at, :]
        rows.append(held)
    for s in range(groups):
        base = k + 8 * s
        half, lane = ("m", base // 128), base % 128
        column = [
            [across_lanes(rows[g][half], lane + t) for t in range(8)] if g >= s else None
            for g in range(groups)
        ]
        pivots = jnp.zeros((8, 128), F32)
        for t in range(8):
            pivot = across_rows(column[s][t], t)
            inverse = reciprocal(pivot)
            pivots = jnp.where(row == t, pivot, pivots)
            pivot_row = {h: across_rows(v, t) for h, v in rows[s].items()}
            entry = [across_rows(column[s][j], t) if j > t else None for j in range(8)]
            for g in range(s, groups):
                factor = column[g][t] * inverse
                if g == s:
                    factor = jnp.where(row > t, factor, 0.0)
                for j in range(t + 1, 8):
                    column[g][j] = column[g][j] - factor * entry[j]
                for h in rows[g]:
                    rows[g][h] = rows[g][h] - factor * pivot_row[h]
        scale = lax.rsqrt(pivots)
        scale = scale * (1.5 - 0.5 * pivots * scale * scale)
        for h in rows[s]:
            rows[s][h] = rows[s][h] * scale
    for g in range(groups):
        at = slice(k + 8 * g, k + 8 * g + 8)
        for (name, h), v in rows[g].items():
            (m_ref if name == "m" else x_ref)[h, at, :] = v


def trailing_step(k, m_ref, x_ref):
    end = k + PANEL
    if end >= RANK:
        return
    m_halves = [h for h in (0, 1) if 128 * (h + 1) > end]
    x_halves = [h for h in (0, 1) if 128 * h < end]
    scaled = jnp.concatenate([m_ref[h, k:end, :] for h in m_halves], axis=1)
    first = 128 * m_halves[0]
    scaled_t = jnp.transpose(scaled)
    other = jnp.concatenate([x_ref[h, k:end, :] for h in x_halves], axis=1)
    for a, b in ((end, end + PANEL), (end + PANEL, RANK)):
        if a >= b:
            continue
        left = scaled_t[a - first : b - first, :]
        change = dot(left, scaled)
        for n, h in enumerate(m_halves):
            m_ref[h, a:b, :] = m_ref[h, a:b, :] - change[:, 128 * n : 128 * n + 128]
        change = dot(left, other)
        for n, h in enumerate(x_halves):
            x_ref[h, a:b, :] = x_ref[h, a:b, :] - change[:, 128 * n : 128 * n + 128]


def kernel(
    grad_ref, momentum_ref, factor_ref, update_ref, out_ref, new_factor_ref,
    grad_v, summed, blocks, blocks_t, gathered, part_tiles, part_in, left_tiles, left_t,
    gram_part, gram_in, m_ref, x_ref, product, product_in, passing, right_p, right_f,
    square_part, square_in,
    load_sem, ring_send, ring_recv, pair_send, pair_recv,
    rs_send, rs_recv, half_send, half_recv, ring2_send, ring2_recv, pair2_send, pair2_recv,
    plane_send, plane_recv, line_send, line_recv, sister_send, sister_recv,
):
    r = lax.axis_index("row")
    c = lax.axis_index("col")
    z = r // 2
    core = lax.rem(r, 2)
    sister = (z * 2 + 1 - core, c)

    def ring(d):
        return lax.rem(z + d + 2 * ZN, ZN)

    toward = ((ring(1) * 2 + core, c), (ring(-1) * 2 + core, c))

    loads = [
        pltpu.make_async_copy(grad_ref, grad_v, load_sem.at[0]),
        pltpu.make_async_copy(momentum_ref, summed, load_sem.at[1]),
    ]
    for load in loads:
        load.start()

    barrier = pltpu.get_barrier_semaphore()

    def greet_line(d, _):
        pl.semaphore_signal(barrier, 1, device_id=(lax.rem(r + d, RN), c), device_id_type=MESH)
        return 0

    def greet_plane(d, _):
        pl.semaphore_signal(barrier, 1, device_id=(r, lax.rem(c + d, CN)), device_id_type=MESH)
        return 0

    lax.fori_loop(1, RN, greet_line, 0)
    lax.fori_loop(1, CN, greet_plane, 0)
    pl.semaphore_wait(barrier, RN - 1 + CN - 1)

    def at(zz, k, lo=0, n=OWN):
        return pl.ds(pl.multiple_of(zz * CHIP + k * OWN + lo, 8), n)

    def ring_gather(buf, sends, recvs, psend, precv):
        def pieces(way, step):
            if step < 4:
                return range(NS)
            return range(CUT) if way == 0 else range(CUT, NS)

        def hop(way, step, s):
            lo, n = SUBS[s]
            zz = ring(-(step - 1)) if way == 0 else ring(step - 1)
            ref = buf.at[at(zz, core, lo, n), :]
            return pltpu.make_async_remote_copy(
                src_ref=ref, dst_ref=ref,
                send_sem=sends.at[way, step - 1, s], recv_sem=recvs.at[way, step - 1, s],
                device_id=toward[way], device_id_type=MESH,
            )

        def over(way, step):
            if step < 4:
                lo, n = 0, OWN
            elif way == 0:
                lo, n = 0, SUBS[CUT][0]
            else:
                lo, n = SUBS[CUT][0], OWN - SUBS[CUT][0]
            zz = ring(-step) if way == 0 else ring(step)
            ref = buf.at[at(zz, core, lo, n), :]
            return pltpu.make_async_remote_copy(
                src_ref=ref, dst_ref=ref,
                send_sem=psend.at[way, step], recv_sem=precv.at[way, step],
                device_id=sister, device_id_type=MESH,
            )

        def start():
            for s in range(NS):
                for way in (0, 1):
                    hop(way, 1, s).start()
            over(0, 0).start()

        def take(step):
            for s in range(NS):
                for way in (0, 1):
                    if s in pieces(way, step):
                        hop(way, step, s).wait_recv()
                        if step < 4 and s in pieces(way, step + 1):
                            hop(way, step + 1, s).start()
            for way in (0, 1):
                over(way, step).start()

        def have(step):
            for way in (0, 1):
                if step > 0 or way == 0:
                    over(way, step).wait_recv()

        def finish():
            for step in range(1, 5):
                for way in (0, 1):
                    for s in pieces(way, step):
                        hop(way, step, s).wait_send()
            over(0, 0).wait_send()
            for step in range(1, 5):
                for way in (0, 1):
                    over(way, step).wait_send()

        return start, take, have, finish

    gathered[at(z, core), :] = factor_ref[...]
    start, take, have, finish = ring_gather(gathered, ring_send, ring_recv, pair_send, pair_recv)
    start()
    for load in loads:
        load.wait()
    for n in range(0, COLS, 128):
        lanes = slice(n, n + 128)
        summed[:, lanes] = summed[:, lanes] + grad_v[:, lanes]
    for b in range(ZN):
        block = summed[:, b * CHIP : (b + 1) * CHIP]
        blocks[b, :, 0:CHIP] = block
    for b in range(ZN):
        blocks_t[b] = jnp.transpose(blocks[b, :, 0:CHIP])

    def partial(zz):
        return dot(blocks[zz, :, 0:CHIP], gathered[pl.ds(pl.multiple_of(zz * CHIP, 8), CHIP), :])

    have(0)
    total = partial(z)
    for step in range(1, 5):
        take(step)
        if step > 1:
            have(step - 1)
            total = total + partial(ring(-(step - 1))) + partial(ring(step - 1))
    have(4)
    total = total + partial(ring(4))
    finish()

    for h in range(2):
        part_tiles[h] = total[:, 128 * h : 128 * h + 128]

    def tile(ref, q):
        return ref.at[q // 16, pl.ds(pl.multiple_of(lax.rem(q, 16) * 8, 8), 8), :]

    def spread(src, dst, index):
        def send(d, _):
            q = lax.rem(c + d, CN)
            pltpu.make_async_remote_copy(
                src_ref=src(q), dst_ref=dst,
                send_sem=plane_send.at[index], recv_sem=plane_recv.at[index],
                device_id=(r, q), device_id_type=MESH,
            ).start()
            return 0

        lax.fori_loop(1, CN, send, 0)

    def plane_wait(sem):
        pltpu.make_async_copy(
            part_in.at[pl.ds(0, CN - 1)], part_in.at[pl.ds(0, CN - 1)], sem
        ).wait()

    part_in[c] = part_tiles[c // 16, pl.ds(pl.multiple_of(lax.rem(c, 16) * 8, 8), 8), :]
    spread(lambda q: tile(part_tiles, q), part_in.at[c], 0)
    plane_wait(plane_recv.at[0])
    own_tile = part_in[0]
    for q in range(1, CN):
        own_tile = own_tile + part_in[q]
    left_tiles[c // 16, pl.ds(pl.multiple_of(lax.rem(c, 16) * 8, 8), 8), :] = own_tile
    spread(lambda q: tile(left_tiles, c), tile(left_tiles, c), 1)
    plane_wait(plane_recv.at[1])
    left = jnp.concatenate([left_tiles[0], left_tiles[1]], axis=1)

    for h in range(2):
        left_t[128 * h : 128 * h + 128, :] = jnp.transpose(left_tiles[h])
    gram_rows = dot(left_t[pl.ds(pl.multiple_of(c * 8, 8), 8), :], left)
    for h in range(2):
        gram_part[h] = gram_rows[:, 128 * h : 128 * h + 128]
    gram_in[r] = gram_part[core]

    def send_line(d, _):
        q = lax.rem(r + d, RN)
        pltpu.make_async_remote_copy(
            src_ref=gram_part.at[lax.rem(q, 2)], dst_ref=gram_in.at[r],
            send_sem=line_send, recv_sem=line_recv,
            device_id=(q, c), device_id_type=MESH,
        ).start()
        return 0

    lax.fori_loop(1, RN, send_line, 0)

    def give(dist):
        zz = ring(dist)
        return pltpu.make_async_remote_copy(
            src_ref=product.at[at(zz, 1 - core), :], dst_ref=product_in.at[zz],
            send_sem=half_send.at[dist], recv_sem=half_recv.at[dist],
            device_id=sister, device_id_type=MESH,
        )

    order = (4, 3, 5, 2, 6, 1, 7, 0)
    for dist in order:
        zz = ring(dist)
        product[pl.ds(pl.multiple_of(zz * CHIP, 8), CHIP), :] = dot(blocks_t[zz], left)
        give(dist).start()

    def add_sister(dist):
        zz = ring(dist)
        give(dist).wait_recv()
        product[at(zz, core), :] = product[at(zz, core), :] + product_in[zz]

    def onward(way, dist, s):
        lo, n = SUBS[s]
        zz = ring(dist) if way == 0 else ring(-dist)
        return pltpu.make_async_remote_copy(
            src_ref=product.at[at(zz, core, lo, n), :],
            dst_ref=passing.at[way, dist - 1, pl.ds(lo, n), :],
            send_sem=rs_send.at[way, dist - 1, s], recv_sem=rs_recv.at[way, dist - 1, s],
            device_id=toward[way], device_id_type=MESH,
        )

    def sub_range(way, dist):
        if dist < 4:
            return range(NS)
        return range(CUT) if way == 0 else range(CUT, NS)

    def scatter_start():
        add_sister(4)
        for s in range(CUT):
            onward(0, 4, s).start()
            onward(1, 4, CUT + s).start()

    def scatter(dist):
        if dist > 0:
            add_sister(dist)
            add_sister(8 - dist)
        else:
            add_sister(0)
        for s in range(NS):
            lo, n = SUBS[s]
            for way in (0, 1):
                zz = ring(dist) if way == 0 else ring(-dist)
                if s in sub_range(way, dist + 1):
                    onward(way, dist + 1, s).wait_recv()
                    rows = at(zz, core, lo, n)
                    product[rows, :] = product[rows, :] + passing[way, dist, lo : lo + n, :]
                if dist > 0:
                    onward(way, dist, s).start()

    def scatter_finish():
        for dist in range(8):
            give(dist).wait_send()
        for dist in range(1, 5):
            for way in (0, 1):
                for s in sub_range(way, dist):
                    onward(way, dist, s).wait_send()

    scatter_start()

    def line_wait(sem):
        pltpu.make_async_copy(
            gram_in.at[pl.ds(0, RN - 1)], gram_in.at[pl.ds(0, RN - 1)], sem
        ).wait()

    line_wait(line_recv)
    gram_tile = gram_in[0]
    for q in range(1, RN):
        gram_tile = gram_tile + gram_in[q]
    gram_at = pl.ds(pl.multiple_of(c * 8, 8), 8)
    m_ref[core, gram_at, :] = gram_tile
    spread(lambda q: m_ref.at[core, gram_at, :], m_ref.at[core, gram_at, :], 2)
    scatter(3)
    plane_wait(plane_recv.at[2])
    to_sister = pltpu.make_async_remote_copy(
        src_ref=m_ref.at[core], dst_ref=m_ref.at[core],
        send_sem=sister_send, recv_sem=sister_recv,
        device_id=sister, device_id_type=MESH,
    )
    to_sister.start()
    row = lax.broadcasted_iota(jnp.int32, (RANK, HALF), 0)
    lane = lax.broadcasted_iota(jnp.int32, (RANK, HALF), 1)
    for h in range(2):
        x_ref[h] = jnp.where(row == lane + 128 * h, 1.0, 0.0).astype(F32)
    plane_wait(plane_send.at[2])
    to_sister.wait()

    start2, take2, have2, finish2 = ring_gather(
        right_p, ring2_send, ring2_recv, pair2_send, pair2_recv
    )

    def own_block():
        scatter(0)
        right_p[at(z, core), :] = product[at(z, core), :]
        start2()

    beside = [
        lambda: scatter(2),
        lambda: scatter(1),
        own_block,
        lambda: take2(1),
        lambda: take2(2),
        lambda: take2(3),
        lambda: take2(4),
    ]
    for n, k in enumerate(range(0, RANK, PANEL)):
        panel_step(k, m_ref, x_ref)
        trailing_step(k, m_ref, x_ref)
        if n < len(beside):
            beside[n]()
    for step in range(5):
        have2(step)

    inverse = jnp.concatenate([x_ref[0], x_ref[1]], axis=1)
    basis = dot_t(left, inverse)

    def right_rows(n, squares):
        rows = pl.ds(pl.multiple_of(n * 128, 128), 128)
        value = dot_t(right_p[rows, :], inverse)
        right_f[rows, :] = value
        square = value * value
        return squares + jnp.sum(square.reshape(16, 8, RANK), axis=0)

    squares = lax.fori_loop(0, COLS // 128, right_rows, jnp.zeros((8, RANK), F32))
    squares = jnp.sum(squares, axis=0, keepdims=True)
    which = lax.broadcasted_iota(jnp.int32, (8, HALF), 0)
    square_tile = jnp.where(which == 0, squares[:, 0:128], squares[:, 128:256])
    square_part[...] = square_tile
    square_in[c] = square_tile
    spread(lambda q: square_part, square_in.at[c], 3)

    for n in range(0, COLS, 128):
        lanes = slice(n, n + 128)
        out_ref[:, lanes] = summed[:, lanes] - feedback * dot_t(basis, right_f[n : n + 128, :])

    plane_wait(plane_recv.at[3])
    square_sum = square_in[0]
    for q in range(1, CN):
        square_sum = square_sum + square_in[q]
    norm = jnp.sqrt(square_sum) + epsilon
    norm = jnp.concatenate([norm[0:1, :], norm[1:2, :]], axis=1)
    new_factor_ref[...] = right_f[at(z, core), :] / norm
    multiplier = math.sqrt(ROWS * RN * COLS * CN / RANK)
    scaled_basis = basis * (multiplier / norm)
    for n in range(0, COLS, 128):
        lanes = slice(n, n + 128)
        update_ref[:, lanes] = dot_t(scaled_basis, right_f[n : n + 128, :])

    for index in (0, 1, 3):
        plane_wait(plane_send.at[index])
    line_wait(line_send)
    scatter_finish()
    finish2()


def per_device(grad, momentum, factor):
    vmem = pl.BlockSpec(memory_space=pltpu.VMEM)
    hbm = pl.BlockSpec(memory_space=pl.ANY)
    dma = pltpu.SemaphoreType.DMA
    out_shape = (
        jax.ShapeDtypeStruct((ROWS, COLS), F32),
        jax.ShapeDtypeStruct((ROWS, COLS), F32),
        jax.ShapeDtypeStruct((OWN, RANK), F32),
    )
    scratch = [
        pltpu.VMEM((ROWS, COLS), F32),
        pltpu.VMEM((ROWS, COLS), F32),
        pltpu.VMEM((ZN, ROWS, 256), F32),
        pltpu.VMEM((ZN, CHIP, ROWS), F32),
        pltpu.VMEM((COLS, RANK), F32),
        pltpu.VMEM((2, ROWS, HALF), F32),
        pltpu.VMEM((CN, 8, HALF), F32),
        pltpu.VMEM((2, ROWS, HALF), F32),
        pltpu.VMEM((RANK, ROWS), F32),
        pltpu.VMEM((2, 8, HALF), F32),
        pltpu.VMEM((RN, 8, HALF), F32),
        pltpu.VMEM((2, RANK, HALF), F32),
        pltpu.VMEM((2, RANK, HALF), F32),
        pltpu.VMEM((COLS, RANK), F32),
        pltpu.VMEM((ZN, OWN, RANK), F32),
        pltpu.VMEM((2, 4, OWN, RANK), F32),
        pltpu.VMEM((COLS, RANK), F32),
        pltpu.VMEM((COLS, RANK), F32),
        pltpu.VMEM((8, HALF), F32),
        pltpu.VMEM((CN, 8, HALF), F32),
        dma((2,)),
        dma((2, 4, NS)), dma((2, 4, NS)),
        dma((2, 5)), dma((2, 5)),
        dma((2, 4, NS)), dma((2, 4, NS)),
        dma((8,)), dma((8,)),
        dma((2, 4, NS)), dma((2, 4, NS)),
        dma((2, 5)), dma((2, 5)),
        dma((4,)), dma((4,)),
        dma, dma,
        dma, dma,
    ]
    return pl.pallas_call(
        kernel,
        out_shape=out_shape,
        in_specs=[hbm, hbm, vmem],
        out_specs=(vmem, vmem, vmem),
        scratch_shapes=scratch,
        compiler_params=pltpu.CompilerParams(
            collective_id=0, has_side_effects=True, vmem_limit_bytes=48 * 1024 * 1024
        ),
    )(grad, momentum, factor)


def solution(mesh):
    return jax.shard_map(
        per_device,
        mesh=mesh,
        in_specs=(P("row", "col"), P("row", "col"), P(("col", "row"), None)),
        out_specs=(P("row", "col"), P("row", "col"), P(("col", "row"), None)),
        check_vma=False,
    )
```

time: 600 us -> 112 us (0.19); the launches traced: 589 us -> 112 us
  waiting for transfers between devices: 434 us -> 0 us
  Pallas kernels: 0 us -> 106 us
  blocking collectives: 60.5 us -> 0 us
  other arithmetic: 58.1 us -> 0 us
  between operations: 15.2 us -> 0.65 us
  matrix products: 14.4 us -> 0 us
    psum x3 -> x0, waiting for transfers between devices: 384 us -> none  [the longest x1 147 us: per_device(): left = lax.psum(partial_left, 'col')]
    pallas_call x0 -> x1, Pallas kernels: none -> 106 us  [per_device(): pl.pallas_call(kernel, out_shape=out_shape, in_specs=[hbm, hbm, vmem], ou...]
    psum x1 -> x0, blocking collectives: 60.5 us -> none  [per_device(): square_sums = lax.psum(jnp.sum(right_factor * right_factor, axis=0), 'col')]
    another operation x9 -> x0, other arithmetic: 53.7 us -> none  [the longest x6 34 us: per_device(): lower_factor = jnp.linalg.cholesky(gram_matrix)]
    all_gather x1 -> x0, waiting for transfers between devices: 49.4 us -> none  [per_device(): local_factor = lax.all_gather(factor, 'row', axis=0, tiled=True)]
    dot_general x5 -> x0, matrix products: 13.1 us -> none  [the longest x1 3.08 us: per_device(): jnp.dot(summed, local_factor, precision=highest, preferred_element_type=j...]
  transfers between devices with their start and end apart: 4 -> 0, of which waited for: 4 -> 0; matrix products, arithmetic and copies ran while one was open for 0% -> 0% of each run, Pallas kernels for 0% -> 0%
where the time goes in v1:
time: 112 us
  Pallas kernels  106 us (95%)
  local copies, waits for them, and re-layouts  5.65 us (5%)
    pallas_call x1, Pallas kernels, per_device(): pl.pallas_call(kernel, out_shape=out_shape, in_specs=[hbm, hbm, vmem], ou...  106 us
    unnamed x9, local copies, waits for them, and re-layouts  5.65 us

profile of v1, /device:TPU:1, one launch (start us, length us, event | category | flops | bytes accessed | tf_op | source)
XLA Modules:
  0.0 111.8 jit_solution(8395147701438858628)
XLA Ops:
  0.6 0.0 copy-start
  0.6 1.1 %copy-done = f32[128,1664]{1,0:T(8,128)S(1)} copy-done((f32[128,1664]{1,0:T(8,128)S(1)}, f32[128,1664]{1,0:T(8,128)}, u32[]{:S(2)}) %copy-start) | copy-done | bytes 851992
  1.8 0.0 copy-start.1
  1.8 1.2 %copy-done.1 = f32[128,1664]{1,0:T(8,128)S(1)} copy-done((f32[128,1664]{1,0:T(8,128)S(1)}, f32[128,1664]{1,0:T(8,128)}, u32[]{:S(2)}) %copy-start.1) | copy-done | bytes 851992
  2.9 0.0 copy-start.2
  2.9 0.9 copy-done.2
  3.8 105.5 %shard_map.58 = (f32[128,1664]{1,0:T(8,128)S(1)}, f32[128,1664]{1,0:T(8,128)S(1)}, f32[104,256]{1,0:T(8,128)S(1)}) custom-call(f32[128,1664]{1,0:T(8,128)S(1)} %copy-done, f32[128,1664]{1,0:T(8,128)S(1)} %copy-done.1, f32[104,256]{1,0:T(8,128)S(1)} %copy-done.2), custom_call_target="tpu_custom_call" | custom-call | tf_op jit(solution)/shard_map/pallas_call | solution.py:514
  109.4 0.9 copy.9
  110.3 0.9 copy.10
  111.2 0.6 copy.11
Async XLA Ops:
  0.6 1.2 %copy-start = (f32[128,1664]{1,0:T(8,128)S(1)}, f32[128,1664]{1,0:T(8,128)}, u32[]{:S(2)}) copy-start(f32[128,1664]{1,0:T(8,128)} %grad_ref.1) | copy-start | bytes 2555908
  1.8 1.2 %copy-start.1 = (f32[128,1664]{1,0:T(8,128)S(1)}, f32[128,1664]{1,0:T(8,128)}, u32[]{:S(2)}) copy-start(f32[128,1664]{1,0:T(8,128)} %momentum_ref.1) | copy-start | bytes 2555908
  2.9 0.9 copy-start.2

commit v2 on v1

v2 whole, which is shorter than its diff:
```python
import functools
import math

import jax
import jax.numpy as jnp
from jax import lax
from jax.experimental import pallas as pl
from jax.experimental.pallas import tpu as pltpu
from jax.sharding import PartitionSpec as P

feedback = 0.05
epsilon = 1e-06
MESH = pl.DeviceIdType.MESH
HIGHEST = lax.Precision.HIGHEST
F32 = jnp.float32
BF16 = jnp.bfloat16

RANK = 256
HALF = 128
ZN = 8
RN = 16
CN = 32
ROWS = 128
COLS = 1664
OWN = COLS // RN
CHIP = 2 * OWN
SUBS = ((0, 32), (32, 24), (56, 24), (80, 24))
NS = len(SUBS)
CUT = 2
PARENT = {1: 0, 2: 1, 3: 2, 4: 2}
SIGN = (1, -1)
LOADS = 4
PANEL = 32


def dot(a, b):
    return jnp.dot(a, b, precision=HIGHEST, preferred_element_type=F32)


def dot_t(a, b):
    return lax.dot_general(
        a, b, (((1,), (1,)), ((), ())), precision=HIGHEST, preferred_element_type=F32
    )


def split(a):
    high = a.astype(BF16)
    return high, (a - high.astype(F32)).astype(BF16)


def split_dot_t(a, b):
    def part(x, y):
        return lax.dot_general(x, y, (((1,), (1,)), ((), ())), preferred_element_type=F32)

    return part(a[0], b[0]) + (part(a[0], b[1]) + part(a[1], b[0]))


def across_rows(x, t):
    return jnp.broadcast_to(x[t : t + 1, :], (8, 128))


def across_lanes(x, t):
    return jnp.broadcast_to(x[:, t : t + 1], (8, 128))


def reciprocal(p):
    r = pltpu.reciprocal(p, approx=True)
    return r * (2.0 - p * r)


def panel_step(k, m_ref, x_ref):
    groups = PANEL // 8
    row = lax.broadcasted_iota(jnp.int32, (8, 128), 0)
    m_halves = [h for h in (0, 1) if 128 * (h + 1) > k]
    x_halves = [h for h in (0, 1) if 128 * h < k + PANEL]
    rows = []
    for g in range(groups):
        at = slice(k + 8 * g, k + 8 * g + 8)
        held = {}
        for h in m_halves:
            held["m", h] = m_ref[h, at, :]
        for h in x_halves:
            held["x", h] = x_ref[h, at, :]
        rows.append(held)
    for s in range(groups):
        base = k + 8 * s
        half, lane = ("m", base // 128), base % 128
        column = [
            [across_lanes(rows[g][half], lane + t) for t in range(8)] if g >= s else None
            for g in range(groups)
        ]
        pivots = jnp.zeros((8, 128), F32)
        for t in range(8):
            pivot = across_rows(column[s][t], t)
            inverse = reciprocal(pivot)
            pivots = jnp.where(row == t, pivot, pivots)
            pivot_row = {h: across_rows(v, t) for h, v in rows[s].items()}
            entry = [across_rows(column[s][j], t) if j > t else None for j in range(8)]
            for g in range(s, groups):
                factor = column[g][t] * inverse
                if g == s:
                    factor = jnp.where(row > t, factor, 0.0)
                for j in range(t + 1, 8):
                    column[g][j] = column[g][j] - factor * entry[j]
                for h in rows[g]:
                    rows[g][h] = rows[g][h] - factor * pivot_row[h]
        scale = lax.rsqrt(pivots)
        scale = scale * (1.5 - 0.5 * pivots * scale * scale)
        for h in rows[s]:
            rows[s][h] = rows[s][h] * scale
    for g in range(groups):
        at = slice(k + 8 * g, k + 8 * g + 8)
        for (name, h), v in rows[g].items():
            (m_ref if name == "m" else x_ref)[h, at, :] = v


def trailing_step(k, m_ref, x_ref):
    end = k + PANEL
    if end >= RANK:
        return
    m_halves = [h for h in (0, 1) if 128 * (h + 1) > end]
    x_halves = [h for h in (0, 1) if 128 * h < end]
    scaled = jnp.concatenate([m_ref[h, k:end, :] for h in m_halves], axis=1)
    first = 128 * m_halves[0]
    scaled_t = jnp.transpose(scaled)
    other = jnp.concatenate([x_ref[h, k:end, :] for h in x_halves], axis=1)
    for a, b in ((end, end + PANEL), (end + PANEL, RANK)):
        if a >= b:
            continue
        left = scaled_t[a - first : b - first, :]
        change = dot(left, scaled)
        for n, h in enumerate(m_halves):
            m_ref[h, a:b, :] = m_ref[h, a:b, :] - change[:, 128 * n : 128 * n + 128]
        change = dot(left, other)
        for n, h in enumerate(x_halves):
            x_ref[h, a:b, :] = x_ref[h, a:b, :] - change[:, 128 * n : 128 * n + 128]


def kernel(
    grad_ref, momentum_ref, factor_ref,
    out_ref, new_factor_ref, basis_ref, right_high, right_low,
    grad_v, summed, blocks, blocks_t, gathered, part_tiles, part_in, left_tiles, left_t,
    gram_part, gram_in, m_ref, x_ref, product, product_in, passing, right_p, own_right,
    square_part, square_in,
    load_sem, ring_send, ring_recv, pair_send, pair_recv,
    rs_send, rs_recv, half_send, half_recv, ring2_send, ring2_recv, pair2_send, pair2_recv,
    plane_send, plane_recv, line_send, line_recv, sister_send, sister_recv,
):
    r = lax.axis_index("row")
    c = lax.axis_index("col")
    z = r // 2
    core = lax.rem(r, 2)
    y = c // 4
    x = lax.rem(c, 4)
    sister = (z * 2 + 1 - core, c)

    def ring(d):
        return lax.rem(z + d + 2 * ZN, ZN)

    def along(d):
        return (ring(d) * 2 + core, c)

    def at(zz, k, lo=0, n=OWN):
        return pl.ds(pl.multiple_of(zz * CHIP + k * OWN + lo, 8), n)

    own_load = pltpu.make_async_copy(
        factor_ref, gathered.at[at(z, core), :], load_sem.at[2 * LOADS]
    )
    own_load.start()
    loads = []
    for n in range(LOADS):
        rows = pl.ds(n * (ROWS // LOADS), ROWS // LOADS)
        for m, (src, dst) in enumerate(((grad_ref, grad_v), (momentum_ref, summed))):
            loads.append(
                pltpu.make_async_copy(src.at[rows, :], dst.at[rows, :], load_sem.at[2 * n + m])
            )
    for load in loads:
        load.start()

    barrier = pltpu.get_barrier_semaphore()

    def greet_line(d, _):
        pl.semaphore_signal(barrier, 1, device_id=(lax.rem(r + d, RN), c), device_id_type=MESH)
        return 0

    def greet_plane(d, _):
        pl.semaphore_signal(barrier, 1, device_id=(r, lax.rem(c + d, CN)), device_id_type=MESH)
        return 0

    lax.fori_loop(1, RN, greet_line, 0)
    lax.fori_loop(1, CN, greet_plane, 0)
    own_load.wait()
    pl.semaphore_wait(barrier, RN - 1 + CN - 1)

    def pieces(dist, way):
        if dist < 4:
            return range(NS)
        return range(CUT) if way == 0 else range(CUT, NS)

    def ring_gather(buf, sends, recvs, psend, precv):
        def hop(way, dist, s):
            lo, n = SUBS[s]
            ref = buf.at[at(ring(-SIGN[way] * PARENT[dist]), core, lo, n), :]
            return pltpu.make_async_remote_copy(
                src_ref=ref, dst_ref=ref,
                send_sem=sends.at[way, dist - 1, s], recv_sem=recvs.at[way, dist - 1, s],
                device_id=along(SIGN[way] * (dist - PARENT[dist])), device_id_type=MESH,
            )

        def over(way, dist):
            if dist < 4:
                lo, n = 0, OWN
            elif way == 0:
                lo, n = 0, SUBS[CUT][0]
            else:
                lo, n = SUBS[CUT][0], OWN - SUBS[CUT][0]
            ref = buf.at[at(ring(-SIGN[way] * dist), core, lo, n), :]
            return pltpu.make_async_remote_copy(
                src_ref=ref, dst_ref=ref,
                send_sem=psend.at[way, dist], recv_sem=precv.at[way, dist],
                device_id=sister, device_id_type=MESH,
            )

        def start(s):
            for way in (0, 1):
                hop(way, 1, s).start()

        def take(dist):
            for s in range(NS):
                for way in (0, 1):
                    if s not in pieces(dist, way):
                        continue
                    hop(way, dist, s).wait_recv()
                    for later in (4, 3, 2):
                        if PARENT[later] == dist and s in pieces(later, way):
                            hop(way, later, s).start()
            for way in (0, 1):
                over(way, dist).start()

        def have(dist):
            for way in (0, 1):
                if dist > 0 or way == 0:
                    over(way, dist).wait_recv()

        def finish():
            over(0, 0).wait_send()
            for dist in range(1, 5):
                for way in (0, 1):
                    over(way, dist).wait_send()
                    for s in pieces(dist, way):
                        hop(way, dist, s).wait_send()

        return start, take, have, finish, over

    start, take, have, finish, over = ring_gather(
        gathered, ring_send, ring_recv, pair_send, pair_recv
    )
    for s in range(NS):
        start(s)
    over(0, 0).start()
    for load in loads:
        load.wait()
    for n in range(0, COLS, 128):
        lanes = slice(n, n + 128)
        summed[:, lanes] = summed[:, lanes] + grad_v[:, lanes]
    for b in range(ZN):
        blocks[b, :, 0:CHIP] = summed[:, b * CHIP : (b + 1) * CHIP]

    def partial(zz):
        return dot(blocks[zz, :, 0:CHIP], gathered[pl.ds(pl.multiple_of(zz * CHIP, 8), CHIP), :])

    take(1)
    have(0)
    total = partial(z)
    take(2)
    have(1)
    total = total + partial(ring(-1)) + partial(ring(1))
    take(3)
    take(4)
    have(2)
    total = total + partial(ring(-2)) + partial(ring(2))
    have(3)
    total = total + partial(ring(-3)) + partial(ring(3))
    have(4)
    total = total + partial(ring(4))

    for h in range(2):
        part_tiles[h] = total[:, 128 * h : 128 * h + 128]

    def tile(ref, q):
        return ref.at[q // 16, pl.ds(pl.multiple_of(lax.rem(q, 16) * 8, 8), 8), :]

    def farthest_first(n, middle):
        return middle + (1 - 2 * lax.rem(n, 2)) * ((n + 1) // 2)

    def spread(src, dst, index):
        def send(dy, dx):
            q = lax.rem(y + dy, 8) * 4 + lax.rem(x + dx, 4)
            pltpu.make_async_remote_copy(
                src_ref=src(q), dst_ref=dst,
                send_sem=plane_send.at[index], recv_sem=plane_recv.at[index],
                device_id=(r, q), device_id_type=MESH,
            ).start()

        def send_row(n, _):
            dy = farthest_first(n, 4)
            for dx in (2, 1, 3, 0):
                send(dy, dx)
            return 0

        lax.fori_loop(0, 7, send_row, 0)
        for dx in (2, 1, 3):
            send(0, dx)

    def plane_wait(sem):
        pltpu.make_async_copy(
            part_in.at[pl.ds(0, CN - 1)], part_in.at[pl.ds(0, CN - 1)], sem
        ).wait()

    spread(lambda q: tile(part_tiles, q), part_in.at[c], 0)
    part_in[c] = part_tiles[c // 16, pl.ds(pl.multiple_of(lax.rem(c, 16) * 8, 8), 8), :]
    for b in range(ZN):
        blocks_t[b] = jnp.transpose(blocks[b, :, 0:CHIP])
    finish()
    plane_wait(plane_recv.at[0])
    own_tile = part_in[0]
    for q in range(1, CN):
        own_tile = own_tile + part_in[q]
    left_tiles[c // 16, pl.ds(pl.multiple_of(lax.rem(c, 16) * 8, 8), 8), :] = own_tile
    spread(lambda q: tile(left_tiles, c), tile(left_tiles, c), 1)
    plane_wait(plane_recv.at[1])
    left = jnp.concatenate([left_tiles[0], left_tiles[1]], axis=1)

    for h in range(2):
        left_t[128 * h : 128 * h + 128, :] = jnp.transpose(left_tiles[h])
    gram_rows = dot(left_t[pl.ds(pl.multiple_of(c * 8, 8), 8), :], left)
    for h in range(2):
        gram_part[h] = gram_rows[:, 128 * h : 128 * h + 128]

    def send_line(q):
        pltpu.make_async_remote_copy(
            src_ref=gram_part.at[lax.rem(q, 2)], dst_ref=gram_in.at[r],
            send_sem=line_send, recv_sem=line_recv,
            device_id=(q, c), device_id_type=MESH,
        ).start()

    def send_chip(n, _):
        zz = ring(farthest_first(n, 4))
        for k in range(2):
            send_line(zz * 2 + k)
        return 0

    lax.fori_loop(0, 7, send_chip, 0)
    send_line(z * 2 + 1 - core)
    gram_in[r] = gram_part[core]

    def give(dist):
        zz = ring(dist)
        return pltpu.make_async_remote_copy(
            src_ref=product.at[at(zz, 1 - core), :], dst_ref=product_in.at[zz],
            send_sem=half_send.at[dist], recv_sem=half_recv.at[dist],
            device_id=sister, device_id_type=MESH,
        )

    def multiply(dist):
        zz = ring(dist)
        product[pl.ds(pl.multiple_of(zz * CHIP, 8), CHIP), :] = dot(blocks_t[zz], left)
        give(dist).start()

    def add_sister(dist):
        zz = ring(dist)
        give(dist).wait_recv()
        product[at(zz, core), :] = product[at(zz, core), :] + product_in[zz]

    def onward(way, dist, s):
        lo, n = SUBS[s]
        return pltpu.make_async_remote_copy(
            src_ref=product.at[at(ring(SIGN[way] * dist), core, lo, n), :],
            dst_ref=passing.at[way, dist - 1, pl.ds(lo, n), :],
            send_sem=rs_send.at[way, dist - 1, s], recv_sem=rs_recv.at[way, dist - 1, s],
            device_id=along(SIGN[way] * (dist - PARENT[dist])), device_id_type=MESH,
        )

    def scatter(dist, after):
        for s in range(NS):
            lo, n = SUBS[s]
            for way in (0, 1):
                rows = at(ring(SIGN[way] * dist), core, lo, n)
                value = product[rows, :]
                for earlier in (3, 4, 2, 1):
                    if PARENT[earlier] == dist and s in pieces(earlier, way):
                        onward(way, earlier, s).wait_recv()
                        value = value + passing[way, earlier - 1, lo : lo + n, :]
                product[rows, :] = value
                if dist > 0:
                    onward(way, dist, s).start()
            after(s)

    def scatter_finish():
        for dist in range(8):
            give(dist).wait_send()
        for dist in range(1, 5):
            for way in (0, 1):
                for s in pieces(dist, way):
                    onward(way, dist, s).wait_send()

    for dist in (4, 3, 5, 2, 6):
        multiply(dist)
    add_sister(4)
    for s in range(CUT):
        onward(0, 4, s).start()
        onward(1, 4, CUT + s).start()
    add_sister(3)
    add_sister(5)
    for s in range(NS):
        for way in (0, 1):
            onward(way, 3, s).start()
    for dist in (1, 7, 0):
        multiply(dist)
    for dist in (2, 6, 1, 7, 0):
        add_sister(dist)

    def line_wait(sem):
        pltpu.make_async_copy(
            gram_in.at[pl.ds(0, RN - 1)], gram_in.at[pl.ds(0, RN - 1)], sem
        ).wait()

    line_wait(line_recv)
    gram_tile = gram_in[0]
    for q in range(1, RN):
        gram_tile = gram_tile + gram_in[q]
    gram_at = pl.ds(pl.multiple_of(c * 8, 8), 8)
    m_ref[core, gram_at, :] = gram_tile
    spread(lambda q: m_ref.at[core, gram_at, :], m_ref.at[core, gram_at, :], 2)
    row = lax.broadcasted_iota(jnp.int32, (RANK, HALF), 0)
    lane = lax.broadcasted_iota(jnp.int32, (RANK, HALF), 1)
    for h in range(2):
        x_ref[h] = jnp.where(row == lane + 128 * h, 1.0, 0.0).astype(F32)

    def nothing(s):
        pass

    scatter(2, nothing)
    scatter(1, nothing)
    plane_wait(plane_recv.at[2])
    to_sister = pltpu.make_async_remote_copy(
        src_ref=m_ref.at[core], dst_ref=m_ref.at[core],
        send_sem=sister_send, recv_sem=sister_recv,
        device_id=sister, device_id_type=MESH,
    )
    to_sister.start()
    start2, take2, have2, finish2, over2 = ring_gather(
        right_p, ring2_send, ring2_recv, pair2_send, pair2_recv
    )

    def gather_piece(s):
        lo, n = SUBS[s]
        rows = at(z, core, lo, n)
        right_p[rows, :] = product[rows, :]
        start2(s)

    scatter(0, gather_piece)
    over2(0, 0).start()
    plane_wait(plane_send.at[2])
    to_sister.wait()

    beside = {1: (1,), 3: (2,), 6: (3, 4)}
    for n, k in enumerate(range(0, RANK, PANEL)):
        panel_step(k, m_ref, x_ref)
        trailing_step(k, m_ref, x_ref)
        for dist in beside.get(n, ()):
            take2(dist)

    inverse = jnp.concatenate([x_ref[0], x_ref[1]], axis=1)

    def right_block(zz, own=False):
        rows = pl.ds(pl.multiple_of(zz * CHIP, 16), CHIP)
        value = dot_t(right_p[rows, :], inverse)
        high, low = split(value)
        right_high[rows, :] = high
        right_low[rows, :] = low
        if own:
            own_right[...] = value
        return jnp.sum((value * value).reshape(CHIP // 8, 8, RANK), axis=0)

    squares = jnp.zeros((8, RANK), F32)
    basis = dot_t(left, inverse)
    for dist in range(5):
        have2(dist)
        if dist == 0:
            squares = squares + right_block(z, own=True)
        elif dist == 4:
            squares = squares + right_block(ring(4))
        else:
            squares = squares + right_block(ring(-dist)) + right_block(ring(dist))
    squares = jnp.sum(squares, axis=0, keepdims=True)
    which = lax.broadcasted_iota(jnp.int32, (8, HALF), 0)
    square_tile = jnp.where(which == 0, squares[:, 0:128], squares[:, 128:256])
    square_part[...] = square_tile
    square_in[c] = square_tile
    spread(lambda q: square_part, square_in.at[c], 3)

    basis_split = split(basis)
    for n in range(0, COLS, 128):
        lanes = slice(n, n + 128)
        right_n = (right_high[lanes, :], right_low[lanes, :])
        out_ref[:, lanes] = summed[:, lanes] - feedback * split_dot_t(basis_split, right_n)
    for index in (0, 1):
        plane_wait(plane_send.at[index])
    line_wait(line_send)
    scatter_finish()
    finish2()

    plane_wait(plane_recv.at[3])
    square_sum = square_in[0]
    for q in range(1, CN):
        square_sum = square_sum + square_in[q]
    norm = jnp.sqrt(square_sum) + epsilon
    norm = jnp.concatenate([norm[0:1, :], norm[1:2, :]], axis=1)
    mine = pl.ds(pl.multiple_of(core * OWN, 8), OWN)
    new_factor_ref[...] = own_right[mine, :] / norm
    multiplier = math.sqrt(ROWS * RN * COLS * CN / RANK)
    basis_ref[...] = basis * (multiplier / norm)
    plane_wait(plane_send.at[3])


def write_kernel(
    momentum_v, factor_v, basis_ref, right_high, right_low, update_ref, out_ref, new_factor_ref,
    update_v, sems,
):
    copies = [pltpu.make_async_copy(factor_v, new_factor_ref, sems.at[0])]
    step = ROWS // LOADS
    for n in range(LOADS):
        rows = pl.ds(n * step, step)
        copies.append(
            pltpu.make_async_copy(momentum_v.at[rows, :], out_ref.at[rows, :], sems.at[1 + n])
        )
    for copy in copies:
        copy.start()
    basis = split(basis_ref[...])
    for i, n in enumerate(range(0, COLS, 128)):
        lanes = slice(n, n + 128)
        update_v[:, lanes] = split_dot_t(basis, (right_high[lanes, :], right_low[lanes, :]))
        copy = pltpu.make_async_copy(
            update_v.at[:, pl.ds(n, 128)], update_ref.at[:, pl.ds(n, 128)], sems.at[1 + LOADS + i]
        )
        copy.start()
        copies.append(copy)
    for copy in copies:
        copy.wait()


def per_device(grad, momentum, factor):
    vmem = pl.BlockSpec(memory_space=pltpu.VMEM)
    hbm = pl.BlockSpec(memory_space=pltpu.HBM)
    dma = pltpu.SemaphoreType.DMA
    out_shape = (
        jax.ShapeDtypeStruct((ROWS, COLS), F32),
        jax.ShapeDtypeStruct((OWN, RANK), F32),
        jax.ShapeDtypeStruct((ROWS, RANK), F32),
        jax.ShapeDtypeStruct((COLS, RANK), BF16),
        jax.ShapeDtypeStruct((COLS, RANK), BF16),
    )
    scratch = [
        pltpu.VMEM((ROWS, COLS), F32),
        pltpu.VMEM((ROWS, COLS), F32),
        pltpu.VMEM((ZN, ROWS, 256), F32),
        pltpu.VMEM((ZN, CHIP, ROWS), F32),
        pltpu.VMEM((COLS, RANK), F32),
        pltpu.VMEM((2, ROWS, HALF), F32),
        pltpu.VMEM((CN, 8, HALF), F32),
        pltpu.VMEM((2, ROWS, HALF), F32),
        pltpu.VMEM((RANK, ROWS), F32),
        pltpu.VMEM((2, 8, HALF), F32),
        pltpu.VMEM((RN, 8, HALF), F32),
        pltpu.VMEM((2, RANK, HALF), F32),
        pltpu.VMEM((2, RANK, HALF), F32),
        pltpu.VMEM((COLS, RANK), F32),
        pltpu.VMEM((ZN, OWN, RANK), F32),
        pltpu.VMEM((2, 4, OWN, RANK), F32),
        pltpu.VMEM((COLS, RANK), F32),
        pltpu.VMEM((CHIP, RANK), F32),
        pltpu.VMEM((8, HALF), F32),
        pltpu.VMEM((CN, 8, HALF), F32),
        dma((2 * LOADS + 1,)),
        dma((2, 4, NS)), dma((2, 4, NS)),
        dma((2, 5)), dma((2, 5)),
        dma((2, 4, NS)), dma((2, 4, NS)),
        dma((8,)), dma((8,)),
        dma((2, 4, NS)), dma((2, 4, NS)),
        dma((2, 5)), dma((2, 5)),
        dma((4,)), dma((4,)),
        dma, dma,
        dma, dma,
    ]
    sent = pl.pallas_call(
        kernel,
        out_shape=out_shape,
        in_specs=[hbm, hbm, hbm],
        out_specs=(vmem,) * 5,
        scratch_shapes=scratch,
        compiler_params=pltpu.CompilerParams(
            collective_id=0, has_side_effects=True, vmem_limit_bytes=52224 * 1024
        ),
    )(grad, momentum, factor)
    full = jax.ShapeDtypeStruct((ROWS, COLS), F32)
    return pl.pallas_call(
        write_kernel,
        out_shape=(full, full, jax.ShapeDtypeStruct((OWN, RANK), F32)),
        in_specs=[vmem] * 5,
        out_specs=(hbm,) * 3,
        scratch_shapes=[pltpu.VMEM((ROWS, COLS), F32), dma((1 + LOADS + COLS // 128,))],
        compiler_params=pltpu.CompilerParams(vmem_limit_bytes=16 * 1024 * 1024),
    )(*sent)


def solution(mesh):
    return jax.shard_map(
        per_device,
        mesh=mesh,
        in_specs=(P("row", "col"), P("row", "col"), P(("col", "row"), None)),
        out_specs=(P("row", "col"), P("row", "col"), P(("col", "row"), None)),
        check_vma=False,
    )
```

time: 112 us -> 88.5 us (0.79); the launches traced: 112 us -> 87 us
  Pallas kernels: 106 us -> 85.3 us
  local copies, waits for them, and re-layouts: 5.65 us -> 0.89 us
    pallas_call x1 -> x2, Pallas kernels: 106 us -> 85.3 us  [the longest x1 83.7 us: per_device(): pl.pallas_call(kernel, out_shape=out_shape, in_specs=[hbm, hbm, hbm], out...]
    unnamed x9 -> x2, local copies, waits for them, and re-layouts: 5.65 us -> 0.89 us
where the time goes in v2:
time: 88.5 us; the launch traced here: 87 us
  Pallas kernels  85.3 us (96%)
  local copies, waits for them, and re-layouts  0.89 us (1%)
    pallas_call x1, Pallas kernels, per_device(): pl.pallas_call(kernel, out_shape=out_shape, in_specs=[hbm, hbm, hbm], out...  83.7 us

profile of v2, /device:TPU:1, one launch (start us, length us, event | category | flops | bytes accessed | tf_op | source)
XLA Modules:
  0.0 87.0 jit_solution(2850486003656926375)
XLA Ops:
  0.6 0.0 copy-start
  0.6 0.9 %copy-done = f32[104,256]{1,0:T(8,128)S(1)} copy-done((f32[104,256]{1,0:T(8,128)S(1)}, f32[104,256]{1,0:T(8,128)}, u32[]{:S(2)}) %copy-start) | copy-done | bytes 106520
  1.5 83.7 %shard_map.58 = (f32[128,1664]{1,0:T(8,128)S(1)}, f32[104,256]{1,0:T(8,128)S(1)}, f32[128,256]{1,0:T(8,128)S(1)}, bf16[1664,256]{1,0:T(8,128)(2,1)S(1)}, bf16[1664,256]{1,0:T(8,128)(2,1)S(1)}) custom-call(f32[128,1664]{1,0:T(8,128)} %grad_ref.1, f32[128,1664]{1,0:T(8,128)} %momentum_ref.1, f32[104,256]{1,0:T(8,128)S(1)} %copy-done), custom_call_target="tpu_custom_call" | custom-call | tf_op jit(solution)/shard_map/pallas_call | solution.py:596
  85.3 1.6 %shard_map.59 = (f32[128,1664]{1,0:T(8,128)}, f32[128,1664]{1,0:T(8,128)}, f32[104,256]{1,0:T(8,128)}) custom-call(f32[128,1664]{1,0:T(8,128)S(1)} %get-tuple-element.8.momentum_v, f32[104,256]{1,0:T(8,128)S(1)} %get-tuple-element.9.factor_v, f32[128,256]{1,0:T(8,128)S(1)} %get-tuple-element.10.basis_ref, ...), custom_call_target="tpu_custom_call" | custom-call | tf_op jit(solution)/shard_map/pallas_call | solution.py:607
Async XLA Ops:
  0.6 0.9 %copy-start = (f32[104,256]{1,0:T(8,128)S(1)}, f32[104,256]{1,0:T(8,128)}, u32[]{:S(2)}) copy-start(f32[104,256]{1,0:T(8,128)} %factor_ref.1) | copy-start | bytes 319492

commit v3 on v2

--- a/solution.py
+++ b/solution.py
@@ -106,12 +106,10 @@
                     rows[g][h] = rows[g][h] - factor * pivot_row[h]
         scale = lax.rsqrt(pivots)
         scale = scale * (1.5 - 0.5 * pivots * scale * scale)
-        for h in rows[s]:
-            rows[s][h] = rows[s][h] * scale
-    for g in range(groups):
-        at = slice(k + 8 * g, k + 8 * g + 8)
-        for (name, h), v in rows[g].items():
-            (m_ref if name == "m" else x_ref)[h, at, :] = v
+        at = slice(k + 8 * s, k + 8 * s + 8)
+        for (name, h), v in rows[s].items():
+            (m_ref if name == "m" else x_ref)[h, at, :] = v * scale
+        yield
 
 
 def trailing_step(k, m_ref, x_ref):
@@ -136,6 +134,13 @@
             x_ref[h, a:b, :] = x_ref[h, a:b, :] - change[:, 128 * n : 128 * n + 128]
 
 
+def inverse_factor(m_ref, x_ref):
+    for k in range(0, RANK, PANEL):
+        yield from panel_step(k, m_ref, x_ref)
+        trailing_step(k, m_ref, x_ref)
+        yield
+
+
 def kernel(
     grad_ref, momentum_ref, factor_ref,
     out_ref, new_factor_ref, basis_ref, right_high, right_low,
@@ -145,6 +150,7 @@
     load_sem, ring_send, ring_recv, pair_send, pair_recv,
     rs_send, rs_recv, half_send, half_recv, ring2_send, ring2_recv, pair2_send, pair2_recv,
     plane_send, plane_recv, line_send, line_recv, sister_send, sister_recv,
+    here_y, here_x,
 ):
     r = lax.axis_index("row")
     c = lax.axis_index("col")
@@ -179,30 +185,69 @@
 
     barrier = pltpu.get_barrier_semaphore()
 
-    def greet_line(d, _):
-        pl.semaphore_signal(barrier, 1, device_id=(lax.rem(r + d, RN), c), device_id_type=MESH)
-        return 0
-
-    def greet_plane(d, _):
-        pl.semaphore_signal(barrier, 1, device_id=(r, lax.rem(c + d, CN)), device_id_type=MESH)
-        return 0
-
-    lax.fori_loop(1, RN, greet_line, 0)
-    lax.fori_loop(1, CN, greet_plane, 0)
-    own_load.wait()
-    pl.semaphore_wait(barrier, RN - 1 + CN - 1)
+    def farthest_first(n, middle):
+        return middle + (1 - 2 * lax.rem(n, 2)) * ((n + 1) // 2)
+
+    def each_of_plane(do):
+        def some(n, _):
+            for dx in (2, 1, 3, 0):
+                do(lax.rem(y + farthest_first(n, 4), 8) * 4 + lax.rem(x + dx, 4))
+            return 0
+
+        lax.fori_loop(0, 7, some, 0)
+        for dx in (2, 1, 3):
+            do(y * 4 + lax.rem(x + dx, 4))
+
+    def each_of_line(do):
+        def some(n, _):
+            for k in range(2):
+                do(ring(farthest_first(n, 4)) * 2 + k)
+            return 0
+
+        lax.fori_loop(0, 7, some, 0)
+        do(z * 2 + 1 - core)
+
+    def greet(device):
+        pl.semaphore_signal(barrier, 1, device_id=device, device_id_type=MESH)
+
+    def beside(dy, dx):
+        return (r, lax.rem(y + dy, 8) * 4 + lax.rem(x + dx, 4))
+
+    in_y = (2, 6, 1, 7)
+    in_x = (2, 1, 3)
+    for d in (2, -2, 1, -1):
+        greet(along(d))
+    for d in in_y:
+        greet(beside(d, 0))
+    for d in in_x:
+        greet(beside(0, d))
+    greet(sister)
+    pl.semaphore_wait(barrier, 12)
+
+    def tell_y():
+        for d in in_y[0:2]:
+            pl.semaphore_signal(
+                here_y, 1, device_id=beside(d, 0), device_id_type=MESH
+            )
+
+    def tell_x():
+        pl.semaphore_wait(here_y, 2)
+        for d in in_x:
+            pl.semaphore_signal(
+                here_x, 1, device_id=beside(0, d), device_id_type=MESH
+            )
 
     def pieces(dist, way):
         if dist < 4:
             return range(NS)
         return range(CUT) if way == 0 else range(CUT, NS)
 
-    def ring_gather(buf, sends, recvs, psend, precv):
+    def ring_gather(buf, own, sends, recvs, psend, precv):
         def hop(way, dist, s):
             lo, n = SUBS[s]
             ref = buf.at[at(ring(-SIGN[way] * PARENT[dist]), core, lo, n), :]
             return pltpu.make_async_remote_copy(
-                src_ref=ref, dst_ref=ref,
+                src_ref=own.at[pl.ds(lo, n), :] if dist == 1 else ref, dst_ref=ref,
                 send_sem=sends.at[way, dist - 1, s], recv_sem=recvs.at[way, dist - 1, s],
                 device_id=along(SIGN[way] * (dist - PARENT[dist])), device_id_type=MESH,
             )
@@ -216,7 +261,7 @@
                 lo, n = SUBS[CUT][0], OWN - SUBS[CUT][0]
             ref = buf.at[at(ring(-SIGN[way] * dist), core, lo, n), :]
             return pltpu.make_async_remote_copy(
-                src_ref=ref, dst_ref=ref,
+                src_ref=own if dist == 0 else ref, dst_ref=ref,
                 send_sem=psend.at[way, dist], recv_sem=precv.at[way, dist],
                 device_id=sister, device_id_type=MESH,
             )
@@ -225,8 +270,8 @@
             for way in (0, 1):
                 hop(way, 1, s).start()
 
-        def take(dist):
-            for s in range(NS):
+        def take(dist, some=range(NS)):
+            for s in some:
                 for way in (0, 1):
                     if s not in pieces(dist, way):
                         continue
@@ -235,7 +280,8 @@
                         if PARENT[later] == dist and s in pieces(later, way):
                             hop(way, later, s).start()
             for way in (0, 1):
-                over(way, dist).start()
+                if pieces(dist, way)[-1] in some:
+                    over(way, dist).start()
 
         def have(dist):
             for way in (0, 1):
@@ -253,13 +299,15 @@
         return start, take, have, finish, over
 
     start, take, have, finish, over = ring_gather(
-        gathered, ring_send, ring_recv, pair_send, pair_recv
+        gathered, factor_ref, ring_send, ring_recv, pair_send, pair_recv
     )
     for s in range(NS):
         start(s)
     over(0, 0).start()
+    tell_y()
     for load in loads:
         load.wait()
+    own_load.wait()
     for n in range(0, COLS, 128):
         lanes = slice(n, n + 128)
         summed[:, lanes] = summed[:, lanes] + grad_v[:, lanes]
@@ -270,6 +318,7 @@
         return dot(blocks[zz, :, 0:CHIP], gathered[pl.ds(pl.multiple_of(zz * CHIP, 8), CHIP), :])
 
     take(1)
+    tell_x()
     have(0)
     total = partial(z)
     take(2)
@@ -284,33 +333,22 @@
     have(4)
     total = total + partial(ring(4))
 
+    pl.semaphore_wait(here_x, 3)
     for h in range(2):
         part_tiles[h] = total[:, 128 * h : 128 * h + 128]
 
     def tile(ref, q):
         return ref.at[q // 16, pl.ds(pl.multiple_of(lax.rem(q, 16) * 8, 8), 8), :]
 
-    def farthest_first(n, middle):
-        return middle + (1 - 2 * lax.rem(n, 2)) * ((n + 1) // 2)
-
     def spread(src, dst, index):
-        def send(dy, dx):
-            q = lax.rem(y + dy, 8) * 4 + lax.rem(x + dx, 4)
+        def send(q):
             pltpu.make_async_remote_copy(
                 src_ref=src(q), dst_ref=dst,
                 send_sem=plane_send.at[index], recv_sem=plane_recv.at[index],
                 device_id=(r, q), device_id_type=MESH,
             ).start()
 
-        def send_row(n, _):
-            dy = farthest_first(n, 4)
-            for dx in (2, 1, 3, 0):
-                send(dy, dx)
-            return 0
-
-        lax.fori_loop(0, 7, send_row, 0)
-        for dx in (2, 1, 3):
-            send(0, dx)
+        each_of_plane(send)
 
     def plane_wait(sem):
         pltpu.make_async_copy(
@@ -331,29 +369,6 @@
     plane_wait(plane_recv.at[1])
     left = jnp.concatenate([left_tiles[0], left_tiles[1]], axis=1)
 
-    for h in range(2):
-        left_t[128 * h : 128 * h + 128, :] = jnp.transpose(left_tiles[h])
-    gram_rows = dot(left_t[pl.ds(pl.multiple_of(c * 8, 8), 8), :], left)
-    for h in range(2):
-        gram_part[h] = gram_rows[:, 128 * h : 128 * h + 128]
-
-    def send_line(q):
-        pltpu.make_async_remote_copy(
-            src_ref=gram_part.at[lax.rem(q, 2)], dst_ref=gram_in.at[r],
-            send_sem=line_send, recv_sem=line_recv,
-            device_id=(q, c), device_id_type=MESH,
-        ).start()
-
-    def send_chip(n, _):
-        zz = ring(farthest_first(n, 4))
-        for k in range(2):
-            send_line(zz * 2 + k)
-        return 0
-
-    lax.fori_loop(0, 7, send_chip, 0)
-    send_line(z * 2 + 1 - core)
-    gram_in[r] = gram_part[core]
-
     def give(dist):
         zz = ring(dist)
         return pltpu.make_async_remote_copy(
@@ -381,8 +396,8 @@
             device_id=along(SIGN[way] * (dist - PARENT[dist])), device_id_type=MESH,
         )
 
-    def scatter(dist, after):
-        for s in range(NS):
+    def scatter(dist, some):
+        for s in some:
             lo, n = SUBS[s]
             for way in (0, 1):
                 rows = at(ring(SIGN[way] * dist), core, lo, n)
@@ -394,7 +409,8 @@
                 product[rows, :] = value
                 if dist > 0:
                     onward(way, dist, s).start()
-            after(s)
+            if dist == 0:
+                gather_piece(s)
 
     def scatter_finish():
         for dist in range(8):
@@ -404,8 +420,35 @@
                 for s in pieces(dist, way):
                     onward(way, dist, s).wait_send()
 
-    for dist in (4, 3, 5, 2, 6):
+    start2, take2, have2, finish2, over2 = ring_gather(
+        right_p, right_p.at[at(z, core), :], ring2_send, ring2_recv, pair2_send, pair2_recv
+    )
+
+    def gather_piece(s):
+        lo, n = SUBS[s]
+        rows = at(z, core, lo, n)
+        right_p[rows, :] = product[rows, :]
+        start2(s)
+
+    for dist in (4, 3, 5):
         multiply(dist)
+
+    for h in range(2):
+        left_t[128 * h : 128 * h + 128, :] = jnp.transpose(left_tiles[h])
+    gram_rows = dot(left_t[pl.ds(pl.multiple_of(c * 8, 8), 8), :], left)
+    for h in range(2):
+        gram_part[h] = gram_rows[:, 128 * h : 128 * h + 128]
+
+    def send_line(q):
+        pltpu.make_async_remote_copy(
+            src_ref=gram_part.at[lax.rem(q, 2)], dst_ref=gram_in.at[r],
+            send_sem=line_send, recv_sem=line_recv,
+            device_id=(q, c), device_id_type=MESH,
+        ).start()
+
+    each_of_line(send_line)
+    gram_in[r] = gram_part[core]
+
     add_sister(4)
     for s in range(CUT):
         onward(0, 4, s).start()
@@ -415,8 +458,12 @@
     for s in range(NS):
         for way in (0, 1):
             onward(way, 3, s).start()
-    for dist in (1, 7, 0):
+    for dist in (2, 6, 1, 7, 0):
         multiply(dist)
+    row = lax.broadcasted_iota(jnp.int32, (RANK, HALF), 0)
+    lane = lax.broadcasted_iota(jnp.int32, (RANK, HALF), 1)
+    for h in range(2):
+        x_ref[h] = jnp.where(row == lane + 128 * h, 1.0, 0.0).astype(F32)
     for dist in (2, 6, 1, 7, 0):
         add_sister(dist)
 
@@ -425,6 +472,7 @@
             gram_in.at[pl.ds(0, RN - 1)], gram_in.at[pl.ds(0, RN - 1)], sem
         ).wait()
 
+    scatter(2, (0, 1))
     line_wait(line_recv)
     gram_tile = gram_in[0]
     for q in range(1, RN):
@@ -432,16 +480,9 @@
     gram_at = pl.ds(pl.multiple_of(c * 8, 8), 8)
     m_ref[core, gram_at, :] = gram_tile
     spread(lambda q: m_ref.at[core, gram_at, :], m_ref.at[core, gram_at, :], 2)
-    row = lax.broadcasted_iota(jnp.int32, (RANK, HALF), 0)
-    lane = lax.broadcasted_iota(jnp.int32, (RANK, HALF), 1)
-    for h in range(2):
-        x_ref[h] = jnp.where(row == lane + 128 * h, 1.0, 0.0).astype(F32)
-
-    def nothing(s):
-        pass
-
-    scatter(2, nothing)
-    scatter(1, nothing)
+    scatter(2, (2, 3))
+    scatter(1, range(NS))
+    scatter(0, (0, 1))
     plane_wait(plane_recv.at[2])
     to_sister = pltpu.make_async_remote_copy(
         src_ref=m_ref.at[core], dst_ref=m_ref.at[core],
@@ -449,27 +490,25 @@
         device_id=sister, device_id_type=MESH,
     )
     to_sister.start()
-    start2, take2, have2, finish2, over2 = ring_gather(
-        right_p, ring2_send, ring2_recv, pair2_send, pair2_recv
-    )
-
-    def gather_piece(s):
-        lo, n = SUBS[s]
-        rows = at(z, core, lo, n)
-        right_p[rows, :] = product[rows, :]
-        start2(s)
-
-    scatter(0, gather_piece)
+    scatter(0, (2, 3))
     over2(0, 0).start()
     plane_wait(plane_send.at[2])
     to_sister.wait()
 
-    beside = {1: (1,), 3: (2,), 6: (3, 4)}
-    for n, k in enumerate(range(0, RANK, PANEL)):
-        panel_step(k, m_ref, x_ref)
-        trailing_step(k, m_ref, x_ref)
-        for dist in beside.get(n, ()):
-            take2(dist)
+    units = inverse_factor(m_ref, x_ref)
+
+    def advance(count):
+        for _ in range(count):
+            next(units, None)
+
+    for before, dists in ((2, (1,)), (6, (2,)), (8, (3, 4))):
+        advance(before)
+        for s in range(NS):
+            for dist in dists:
+                take2(dist, (s,))
+            advance(2)
+    for _ in units:
+        pass
 
     inverse = jnp.concatenate([x_ref[0], x_ref[1]], axis=1)
 
@@ -592,6 +631,7 @@
         dma((4,)), dma((4,)),
         dma, dma,
         dma, dma,
+        pltpu.SemaphoreType.REGULAR, pltpu.SemaphoreType.REGULAR,
     ]
     sent = pl.pallas_call(
         kernel,

time: 88.5 us -> 85.8 us (0.969)
  Pallas kernels: 85.3 us -> 83.5 us
    pallas_call x1, Pallas kernels: 83.7 us -> 81.9 us  [per_device(): pl.pallas_call(kernel, out_shape=out_shape, in_specs=[hbm, hbm, hbm], out...]
where the time goes in v3:
time: 85.8 us; the launch traced here: 85.2 us
  Pallas kernels  83.5 us (97%)
  local copies, waits for them, and re-layouts  0.89 us (1%)
    pallas_call x1, Pallas kernels, per_device(): pl.pallas_call(kernel, out_shape=out_shape, in_specs=[hbm, hbm, hbm], out...  81.9 us

profile of v3, /device:TPU:1, one launch (start us, length us, event | category | flops | bytes accessed | tf_op | source)
XLA Modules:
  0.0 85.2 jit_solution(7697285920642709550)
XLA Ops:
  0.6 0.0 copy-start
  0.6 0.9 %copy-done = f32[104,256]{1,0:T(8,128)S(1)} copy-done((f32[104,256]{1,0:T(8,128)S(1)}, f32[104,256]{1,0:T(8,128)}, u32[]{:S(2)}) %copy-start) | copy-done | bytes 106520
  1.5 81.9 %shard_map.58 = (f32[128,1664]{1,0:T(8,128)S(1)}, f32[104,256]{1,0:T(8,128)S(1)}, f32[128,256]{1,0:T(8,128)S(1)}, bf16[1664,256]{1,0:T(8,128)(2,1)S(1)}, bf16[1664,256]{1,0:T(8,128)(2,1)S(1)}) custom-call(f32[128,1664]{1,0:T(8,128)} %grad_ref.1, f32[128,1664]{1,0:T(8,128)} %momentum_ref.1, f32[104,256]{1,0:T(8,128)S(1)} %copy-done), custom_call_target="tpu_custom_call" | custom-call | tf_op jit(solution)/shard_map/pallas_call | solution.py:636
  83.4 1.6 %shard_map.59 = (f32[128,1664]{1,0:T(8,128)}, f32[128,1664]{1,0:T(8,128)}, f32[104,256]{1,0:T(8,128)}) custom-call(f32[128,1664]{1,0:T(8,128)S(1)} %get-tuple-element.8.momentum_v, f32[104,256]{1,0:T(8,128)S(1)} %get-tuple-element.9.factor_v, f32[128,256]{1,0:T(8,128)S(1)} %get-tuple-element.10.basis_ref, ...), custom_call_target="tpu_custom_call" | custom-call | tf_op jit(solution)/shard_map/pallas_call | solution.py:647
Async XLA Ops:
  0.6 0.9 %copy-start = (f32[104,256]{1,0:T(8,128)S(1)}, f32[104,256]{1,0:T(8,128)}, u32[]{:S(2)}) copy-start(f32[104,256]{1,0:T(8,128)} %factor_ref.1) | copy-start | bytes 319492

commit v4 on v3

--- a/solution.py
+++ b/solution.py
@@ -46,6 +46,21 @@
 def split(a):
     high = a.astype(BF16)
     return high, (a - high.astype(F32)).astype(BF16)
+
+
+def split3(a):
+    high = a.astype(BF16)
+    rest = a - high.astype(F32)
+    middle = rest.astype(BF16)
+    return high, middle, (rest - middle.astype(F32)).astype(BF16)
+
+
+def split3_dot(a, b):
+    def part(x, y):
+        return jnp.dot(x, y, preferred_element_type=F32)
+
+    small = (part(a[1], b[1]) + part(a[0], b[2])) + part(a[2], b[0])
+    return part(a[0], b[0]) + ((part(a[0], b[1]) + part(a[1], b[0])) + small)
 
 
 def split_dot_t(a, b):
@@ -449,14 +464,12 @@
     each_of_line(send_line)
     gram_in[r] = gram_part[core]
 
-    add_sister(4)
-    for s in range(CUT):
-        onward(0, 4, s).start()
-        onward(1, 4, CUT + s).start()
-    add_sister(3)
-    add_sister(5)
+    for dist in (4, 3, 5):
+        add_sister(dist)
     for s in range(NS):
         for way in (0, 1):
+            if s in pieces(4, way):
+                onward(way, 4, s).start()
             onward(way, 3, s).start()
     for dist in (2, 6, 1, 7, 0):
         multiply(dist)
@@ -512,9 +525,11 @@
 
     inverse = jnp.concatenate([x_ref[0], x_ref[1]], axis=1)
 
+    inverse_t = split3(jnp.transpose(inverse))
+
     def right_block(zz, own=False):
         rows = pl.ds(pl.multiple_of(zz * CHIP, 16), CHIP)
-        value = dot_t(right_p[rows, :], inverse)
+        value = split3_dot(split3(right_p[rows, :]), inverse_t)
         high, low = split(value)
         right_high[rows, :] = high
         right_low[rows, :] = low

time: 85.8 us -> 84.8 us (0.988)
  no operation moved by 1% of the time
where the time goes in v4:
time: 84.8 us; the launch traced here: 84.7 us
  Pallas kernels  83 us (98%)
  local copies, waits for them, and re-layouts  0.89 us (1%)
    pallas_call x1, Pallas kernels, per_device(): pl.pallas_call(kernel, out_shape=out_shape, in_specs=[hbm, hbm, hbm], out...  81.4 us

profile of v4, /device:TPU:1, one launch (start us, length us, event | category | flops | bytes accessed | tf_op | source)
XLA Modules:
  0.0 84.7 jit_solution(10624380489549133366)
XLA Ops:
  0.6 0.0 copy-start
  0.6 0.9 %copy-done = f32[104,256]{1,0:T(8,128)S(1)} copy-done((f32[104,256]{1,0:T(8,128)S(1)}, f32[104,256]{1,0:T(8,128)}, u32[]{:S(2)}) %copy-start) | copy-done | bytes 106520
  1.5 81.4 %shard_map.58 = (f32[128,1664]{1,0:T(8,128)S(1)}, f32[104,256]{1,0:T(8,128)S(1)}, f32[128,256]{1,0:T(8,128)S(1)}, bf16[1664,256]{1,0:T(8,128)(2,1)S(1)}, bf16[1664,256]{1,0:T(8,128)(2,1)S(1)}) custom-call(f32[128,1664]{1,0:T(8,128)} %grad_ref.1, f32[128,1664]{1,0:T(8,128)} %momentum_ref.1, f32[104,256]{1,0:T(8,128)S(1)} %copy-done), custom_call_target="tpu_custom_call" | custom-call | tf_op jit(solution)/shard_map/pallas_call | solution.py:651
  82.9 1.6 %shard_map.59 = (f32[128,1664]{1,0:T(8,128)}, f32[128,1664]{1,0:T(8,128)}, f32[104,256]{1,0:T(8,128)}) custom-call(f32[128,1664]{1,0:T(8,128)S(1)} %get-tuple-element.8.momentum_v, f32[104,256]{1,0:T(8,128)S(1)} %get-tuple-element.9.factor_v, f32[128,256]{1,0:T(8,128)S(1)} %get-tuple-element.10.basis_ref, ...), custom_call_target="tpu_custom_call" | custom-call | tf_op jit(solution)/shard_map/pallas_call | solution.py:662
Async XLA Ops:
  0.6 0.9 %copy-start = (f32[104,256]{1,0:T(8,128)S(1)}, f32[104,256]{1,0:T(8,128)}, u32[]{:S(2)}) copy-start(f32[104,256]{1,0:T(8,128)} %factor_ref.1) | copy-start | bytes 319492

commit v5 on v4

--- a/solution.py
+++ b/solution.py
@@ -320,6 +320,11 @@
         start(s)
     over(0, 0).start()
     tell_y()
+    def partial(zz):
+        return dot(blocks[zz, :, 0:CHIP], gathered[pl.ds(pl.multiple_of(zz * CHIP, 8), CHIP), :])
+
+    take(1)
+    tell_x()
     for load in loads:
         load.wait()
     own_load.wait()
@@ -328,12 +333,6 @@
         summed[:, lanes] = summed[:, lanes] + grad_v[:, lanes]
     for b in range(ZN):
         blocks[b, :, 0:CHIP] = summed[:, b * CHIP : (b + 1) * CHIP]
-
-    def partial(zz):
-        return dot(blocks[zz, :, 0:CHIP], gathered[pl.ds(pl.multiple_of(zz * CHIP, 8), CHIP), :])
-
-    take(1)
-    tell_x()
     have(0)
     total = partial(z)
     take(2)
@@ -514,12 +513,12 @@
         for _ in range(count):
             next(units, None)
 
-    for before, dists in ((2, (1,)), (6, (2,)), (8, (3, 4))):
+    for before, dists in ((2, (1,)), (6, (2,)), (11, (3, 4))):
         advance(before)
         for s in range(NS):
             for dist in dists:
                 take2(dist, (s,))
-            advance(2)
+            advance(2 if dists[0] < 3 else 1)
     for _ in units:
         pass
 

time: 84.8 us -> 84.5 us (level)
  no operation moved by 1% of the time
where the time goes in v5:
time: 84.5 us; the launch traced here: 84.3 us
  Pallas kernels  82.6 us (98%)
  local copies, waits for them, and re-layouts  0.89 us (1%)
    pallas_call x1, Pallas kernels, per_device(): pl.pallas_call(kernel, out_shape=out_shape, in_specs=[hbm, hbm, hbm], out...  81 us

profile of v5, /device:TPU:1, one launch (start us, length us, event | category | flops | bytes accessed | tf_op | source)
XLA Modules:
  0.0 84.3 jit_solution(10849717630076075853)
XLA Ops:
  0.6 0.0 copy-start
  0.6 0.9 %copy-done = f32[104,256]{1,0:T(8,128)S(1)} copy-done((f32[104,256]{1,0:T(8,128)S(1)}, f32[104,256]{1,0:T(8,128)}, u32[]{:S(2)}) %copy-start) | copy-done | bytes 106520
  1.5 81.0 %shard_map.58 = (f32[128,1664]{1,0:T(8,128)S(1)}, f32[104,256]{1,0:T(8,128)S(1)}, f32[128,256]{1,0:T(8,128)S(1)}, bf16[1664,256]{1,0:T(8,128)(2,1)S(1)}, bf16[1664,256]{1,0:T(8,128)(2,1)S(1)}) custom-call(f32[128,1664]{1,0:T(8,128)} %grad_ref.1, f32[128,1664]{1,0:T(8,128)} %momentum_ref.1, f32[104,256]{1,0:T(8,128)S(1)} %copy-done), custom_call_target="tpu_custom_call" | custom-call | tf_op jit(solution)/shard_map/pallas_call | solution.py:650
  82.5 1.6 %shard_map.59 = (f32[128,1664]{1,0:T(8,128)}, f32[128,1664]{1,0:T(8,128)}, f32[104,256]{1,0:T(8,128)}) custom-call(f32[128,1664]{1,0:T(8,128)S(1)} %get-tuple-element.8.momentum_v, f32[104,256]{1,0:T(8,128)S(1)} %get-tuple-element.9.factor_v, f32[128,256]{1,0:T(8,128)S(1)} %get-tuple-element.10.basis_ref, ...), custom_call_target="tpu_custom_call" | custom-call | tf_op jit(solution)/shard_map/pallas_call | solution.py:661
Async XLA Ops:
  0.6 0.9 %copy-start = (f32[104,256]{1,0:T(8,128)S(1)}, f32[104,256]{1,0:T(8,128)}, u32[]{:S(2)}) copy-start(f32[104,256]{1,0:T(8,128)} %factor_ref.1) | copy-start | bytes 319492
